TPU v7x, 32 devices: a whole 2x2x4 slice. The times are simulated.
32 devices in a mesh: sx: 4 (over y, core), sy: 8 (over z, x).
Axes of the slice: x: 2, y: 2, z: 4, core: 2. Of those that a mesh axis runs over, the one named last changes fastest.
Arguments:
- loads: float32 [4, 8, 1536, 256], P('sx', 'sy')
- schur_flex: float32 [4, 8, 1536, 1536], P('sx', 'sy'), as said below
- dirichlet: float32 [4, 8, 1536, 1536], P('sx', 'sy'), as said below
- coupling: float32 [4, 8, 16, 1536], P('sx', 'sy'), may hold values from -0.3125 to 0.3125
- corner_index: int32 [4, 8, 16], P('sx', 'sy'), may hold values from 0 to 128, as said below
- face_lists: int32 [4, 8, 4, 384], P('sx', 'sy'), may hold values from 0 to 383, as said below
- coarse_inverse: float32 [128, 128], P(('sx', 'sy')), as said below
Outputs:
- multipliers: float32 [4, 8, 1536, 256], P('sx', 'sy')
- residual: float32 [4, 8, 1536, 256], P('sx', 'sy')
Inputs may be any that keep to these rules, and one draw needn't show every extreme that they name: `corner_index`: each subdomain lists 4 coarse dofs for each of its four corners; 128 marks a corner on the clamped edges of the panel, which has no coarse dof; every coarse dof below 128 is named by some subdomain. `face_lists`: each face's list is a permutation of the 384 dofs of the facing face; the facing lists of two neighbouring subdomains are inverse permutations. `schur_flex`: symmetric positive definite for every subdomain. `dirichlet`: symmetric positive definite for every subdomain. `coarse_inverse`: symmetric positive definite.
All inputs are finite; a program needn't handle non-finite values.
Results may differ from a plain program's by a relative error of at most 0.00017.
Values sent between devices are 32-bit elements; how exact they have to be, the bound alone decides.
No kernel may reach another device: no remote copies, remote signals or barrier semaphores. Data moves between devices by JAX's collectives and lax.ppermute only.
A program may use at most 128 MiB of HBM per device.

v0:
```python
import jax
import jax.numpy as jnp
from jax import lax
from jax.sharding import PartitionSpec as P

ITERS = 2


def shifted(block, axis, distance):
    devices = range(lax.axis_size(axis))
    route = [(i - distance, i) for i in devices if i - distance in devices]
    return lax.ppermute(block, axis, route)


def jump(field, face_index):
    size = field.shape[0] // 4
    width = field.shape[1]
    face_rows = field.reshape(4, size, width)
    from_low_x = shifted(face_rows[1], "sx", 1)
    from_high_x = shifted(face_rows[0], "sx", -1)
    from_low_y = shifted(face_rows[3], "sy", 1)
    from_high_y = shifted(face_rows[2], "sy", -1)
    received = jnp.stack([from_low_x, from_high_x, from_low_y, from_high_y], axis=0)
    matched = received[jnp.arange(4, dtype=jnp.int32)[:, None], face_index]
    return (face_rows - matched).reshape(4 * size, width)


def coarse_solve(coarse_rhs, matrix_all):
    highest = lax.Precision.HIGHEST
    total = lax.psum(coarse_rhs, ("sx", "sy"))
    return jnp.dot(matrix_all, total, precision=highest)


def inner(first, second):
    return jnp.sum(first * second, axis=0)


def shards(loads, schur_flex, dirichlet, coupling, corner_index, face_lists, coarse_inverse):
    highest = lax.Precision.HIGHEST
    flex_mat = schur_flex[0, 0]
    prec_mat = dirichlet[0, 0]
    coupling_mat = coupling[0, 0]
    corners = corner_index[0, 0]
    face_index = face_lists[0, 0]
    ncoarse = coarse_inverse.shape[1]
    onehot = (corners[None, :] == jnp.arange(ncoarse, dtype=jnp.int32)[:, None]).astype(jnp.float32)
    matrix_all = lax.all_gather(coarse_inverse, ("sx", "sy"), axis=0, tiled=True)

    def precondition(dual_vector):
        spread = jump(dual_vector, face_index)
        operator_applied = jnp.dot(prec_mat, spread, precision=highest)
        return 0.5 * jump(operator_applied, face_index)

    def residual_dot(residual, precond):
        return lax.psum(inner(residual, precond), ("sx", "sy"))

    force_discontinuity = jump(loads[0, 0], face_index)
    multipliers = jnp.zeros_like(force_discontinuity)
    residual = force_discontinuity
    precond = precondition(residual)
    direction = precond
    residual_inner = residual_dot(residual, precond)
    for iteration in range(ITERS):
        width = direction.shape[1]
        apply_spread = jump(direction, face_index)
        fine_part = jnp.dot(flex_mat, apply_spread, precision=highest)
        local_load = jnp.dot(coupling_mat, apply_spread, precision=highest)
        coarse_rhs = jnp.dot(onehot, local_load, precision=highest)
        coarse_sol = coarse_solve(coarse_rhs, matrix_all)
        filled_out = jnp.concatenate([coarse_sol, jnp.zeros((1, width), jnp.float32)], axis=0)
        picked = filled_out[corners]
        correction = lax.dot_general(
            coupling_mat, picked, (((0,), (0,)), ((), ())), precision=highest
        )
        image_dir = jump(fine_part + correction, face_index)
        step_size = residual_inner / lax.psum(inner(direction, image_dir), ("sx", "sy"))
        multipliers = multipliers + step_size * direction
        residual = residual - step_size * image_dir
        if iteration + 1 < ITERS:
            precond = precondition(residual)
            new_dot = residual_dot(residual, precond)
            direction = precond + new_dot / residual_inner * direction
            residual_inner = new_dot
    return (multipliers[None, None], residual[None, None])


def solution(mesh):
    return jax.shard_map(
        shards,
        mesh=mesh,
        in_specs=(
            P("sx", "sy", None, None),
            P("sx", "sy", None, None),
            P("sx", "sy", None, None),
            P("sx", "sy", None, None),
            P("sx", "sy", None),
            P("sx", "sy", None, None),
            P(("sx", "sy"), None),
        ),
        out_specs=(P("sx", "sy", None, None), P("sx", "sy", None, None)),
        check_vma=False,
    )
```

profile of v0, /device:TPU:0, one launch (start us, length us, event | category | flops | bytes accessed | tf_op | source)
XLA Modules:
  0.0 960.7 jit_solution(12696364601116534008)
XLA Ops:
  12.4 4.2 collective-permute-start.2
  18.0 15.0 %collective-permute-done.2 = f32[384,256]{1,0:T(8,128)S(1)} collective-permute-done((f32[384,256]{1,0:T(8,128)S(1)}, f32[384,256]{1,0:T(8,128)S(1)}, u32[]{:S(2)}, u32[]{:S(2)}) %collective-permute-start.2) | collective-permute-done | bytes 393248 | tf_op jit(solution)/shard_map/ppermute | solution.py:12
  33.2 18.0 %gather_fusion = f32[1536,256]{1,0:T(8,128)} fusion(f32[4,384,256]{2,1,0:T(8,128)S(1)} %pad_maximum_fusion, s32[1536]{0:T(1024)S(1)} %reshape.175), kind=kCustom, calls=%fused_computation | custom fusion | bytes 3158016 | tf_op jit(solution)/shard_map/gather | solution.py:24
  54.1 3.5 collective-permute-start.4
  59.0 4.1 collective-permute-start.6
  64.4 14.7 %collective-permute-done.6 = f32[384,256]{1,0:T(8,128)S(1)} collective-permute-done((f32[384,256]{1,0:T(8,128)S(1)}, f32[384,256]{1,0:T(8,128)S(1)}, u32[]{:S(2)}, u32[]{:S(2)}) %collective-permute-start.6) | collective-permute-done | bytes 393248 | tf_op jit(solution)/shard_map/ppermute | solution.py:12
  79.3 18.0 %gather_fusion.1 = f32[1536,256]{1,0:T(8,128)} fusion(f32[4,384,256]{2,1,0:T(8,128)S(1)} %pad_maximum_fusion.1, s32[1536]{0:T(1024)S(1)} %reshape.175), kind=kCustom, calls=%fused_computation.1 | custom fusion | bytes 3158016 | tf_op jit(solution)/shard_map/gather | solution.py:24
  99.1 18.2 %fusion.10 = f32[1536,256]{0,1:T(8,128)S(1)} fusion(f32[1536,256]{1,0:T(8,128)S(1)} %bitcast.124, f32[1,1,1536,1536]{3,2,1,0:T(8,128)} %param.9), kind=kOutput, calls=%fused_computation.23 | convolution fusion | flops 7247757312 | bytes 12582912 | tf_op jit(solution)/shard_map/dot_general | solution.py:51
  117.3 3.9 collective-permute-start.8
  122.5 4.1 collective-permute-start.10
  128.2 5.7 collective-permute-done.10
  133.9 6.5 collective-permute-done.11
  143.6 18.0 %gather_fusion.2 = f32[1536,256]{1,0:T(8,128)} fusion(f32[4,384,256]{2,1,0:T(8,128)S(1)} %copy.27, s32[1536]{0:T(1024)S(1)} %reshape.175), kind=kCustom, calls=%fused_computation.2 | custom fusion | bytes 3158016 | tf_op jit(solution)/shard_map/gather | solution.py:24
  166.6 6.2 collective-permute-start.12
  174.1 4.1 collective-permute-start.14
  179.5 78.8 %all-gather = f32[32,4,128]{2,1,0:T(4,128)S(1)} all-gather(f32[1,4,128]{2,1,0:T(4,128)S(1)} %bitcast.161), channel_id=1, replica_groups=mesh['sx'=4,'sy'=8] {'sx','sy'}, dimensions={0}, use_global_device_ids=true | all-gather | bytes 67584 | tf_op jit(solution)/shard_map/all_gather | solution.py:47
  261.5 18.0 %gather_fusion.3 = f32[1536,256]{1,0:T(8,128)} fusion(f32[4,384,256]{2,1,0:T(8,128)S(1)} %copy.31, s32[1536]{0:T(1024)S(1)} %reshape.175), kind=kCustom, calls=%fused_computation.3 | custom fusion | bytes 3158016 | tf_op jit(solution)/shard_map/gather | solution.py:24
  283.7 11.6 %fusion.2 = f32[256,1536]{1,0:T(8,128)} fusion(f32[1,1,1536,1536]{3,2,1,0:T(8,128)} %param.8, f32[1536,256]{0,1:T(8,128)S(1)} %copy.32, f32[1536,256]{0,1:T(8,128)S(1)} %get-tuple-element.16), kind=kOutput, calls=%fused_computation.13 | convolution fusion | flops 7248543744 | bytes 14155776 | tf_op jit(solution)/shard_map/dot_general | solution.py:66
  295.3 109.0 %all-reduce.6.cloned.1.call-done = f32[128,256]{1,0:T(8,128)} async-done(((f32[128,256]{1,0:T(8,128)}), f32[128,256]{1,0:T(8,128)}) %all-reduce.6.cloned.1.call-update) | async-done | bytes 131088 | tf_op jit(solution)/shard_map/psum | solution.py:30
  414.0 4.1 collective-permute-start.18
  418.1 11.6 %collective-permute-start.19 = (f32[384,256]{0,1:T(8,128)}, f32[384,256]{0,1:T(8,128)}, u32[]{:S(2)}, u32[]{:S(2)}) collective-permute-start(f32[384,256]{0,1:T(8,128)} %get-tuple-element.34), channel_id=1, source_target_pairs={{1,0},{2,1},{3,2},{4,3},{5,4},{6,5},{7,6},{9,8},{10,9},{11,10},{12... | collective-permute-start | bytes 1179656 | tf_op jit(solution)/shard_map/ppermute | solution.py:12
  439.0 18.0 %gather_fusion.5 = f32[1536,256]{1,0:T(8,128)} fusion(f32[4,384,256]{2,1,0:T(8,128)S(1)} %copy.33, s32[1536]{0:T(1024)S(1)} %reshape.175), kind=kCustom, calls=%fused_computation.5 | custom fusion | bytes 3158016 | tf_op jit(solution)/shard_map/gather | solution.py:24
  457.0 3.2 copy.34
  460.1 3.8 multiply_reduce_fusion.2
  464.0 42.4 %all-reduce.2 = (f32[256]{0:T(256)S(1)}, f32[256]{0:T(256)S(1)}) all-reduce(f32[256]{0:T(256)S(1)} %get-tuple-element.7, f32[256]{0:T(256)S(1)} %get-tuple-element.6), channel_id=1, replica_groups=mesh['sx'=4,'sy'=8] {'sx','sy'}, use_global_device_ids=true, to_apply=%region_1.0 | all-reduce | flops 512 | bytes 4096 | tf_op jit(solution)/shard_map/psum | solution.py:55
  512.8 4.4 collective-permute-start.22
  518.5 14.3 %collective-permute-done.22 = f32[384,256]{0,1:T(8,128)S(1)} collective-permute-done((f32[384,256]{0,1:T(8,128)S(1)}, f32[384,256]{0,1:T(8,128)S(1)}, u32[]{:S(2)}, u32[]{:S(2)}) %collective-permute-start.22) | collective-permute-done | bytes 393248 | tf_op jit(solution)/shard_map/ppermute | solution.py:12
  535.9 18.0 %gather_fusion.6 = f32[1536,256]{1,0:T(8,128)} fusion(f32[4,384,256]{2,1,0:T(8,128)S(1)} %copy.35, s32[1536]{0:T(1024)S(1)} %reshape.175), kind=kCustom, calls=%fused_computation.6 | custom fusion | bytes 3158016 | tf_op jit(solution)/shard_map/gather | solution.py:24
  554.0 3.2 copy.36
  557.2 11.3 %fusion.13 = f32[1536,256]{0,1:T(8,128)S(1)} fusion(f32[1,1,1536,1536]{3,2,1,0:T(8,128)} %param.9, f32[1536,256]{0,1:T(8,128)S(1)} %copy-done.5, f32[1536,256]{0,1:T(8,128)} %copy.36), kind=kOutput, calls=%fused_computation.24 | convolution fusion | flops 7248150528 | bytes 14155776 | tf_op jit(solution)/shard_map/dot_general | solution.py:51
  569.6 4.3 collective-permute-start.24
  575.2 4.1 collective-permute-start.26
  580.7 14.0 %collective-permute-done.26 = f32[384,256]{0,1:T(8,128)S(1)} collective-permute-done((f32[384,256]{0,1:T(8,128)S(1)}, f32[384,256]{0,1:T(8,128)S(1)}, u32[]{:S(2)}, u32[]{:S(2)}) %collective-permute-start.26) | collective-permute-done | bytes 393248 | tf_op jit(solution)/shard_map/ppermute | solution.py:12
  597.8 18.0 %gather_fusion.7 = f32[1536,256]{1,0:T(8,128)} fusion(f32[4,384,256]{2,1,0:T(8,128)S(1)} %copy.37, s32[1536]{0:T(1024)S(1)} %reshape.175), kind=kCustom, calls=%fused_computation.7 | custom fusion | bytes 3158016 | tf_op jit(solution)/shard_map/gather | solution.py:24
  615.8 3.1 copy.38
  621.3 45.1 %psum.45 = f32[256]{0:T(256)S(1)} all-reduce(f32[256]{0:T(256)S(1)} %multiply_reduce_fusion.1), channel_id=1, replica_groups=mesh['sx'=4,'sy'=8] {'sx','sy'}, use_global_device_ids=true, to_apply=%region_6.0 | all-reduce | flops 256 | bytes 2048 | tf_op jit(solution)/shard_map/psum | solution.py:55
  672.3 4.4 collective-permute-start.30
  678.2 14.1 %collective-permute-done.30 = f32[384,256]{0,1:T(8,128)S(1)} collective-permute-done((f32[384,256]{0,1:T(8,128)S(1)}, f32[384,256]{0,1:T(8,128)S(1)}, u32[]{:S(2)}, u32[]{:S(2)}) %collective-permute-start.30) | collective-permute-done | bytes 393248 | tf_op jit(solution)/shard_map/ppermute | solution.py:12
  695.5 18.0 %gather_fusion.8 = f32[1536,256]{1,0:T(8,128)} fusion(f32[4,384,256]{2,1,0:T(8,128)S(1)} %copy.39, s32[1536]{0:T(1024)S(1)} %reshape.175), kind=kCustom, calls=%fused_computation.8 | custom fusion | bytes 3158016 | tf_op jit(solution)/shard_map/gather | solution.py:24
  713.4 3.2 copy.40
  720.3 12.2 %fusion = f32[256,1536]{1,0:T(8,128)} fusion(f32[1,1,1536,1536]{3,2,1,0:T(8,128)} %param.8, f32[1536,256]{0,1:T(8,128)S(1)} %copy-done.2, f32[1536,256]{0,1:T(8,128)} %copy.40), kind=kOutput, calls=%fused_computation.11 | convolution fusion | flops 7248150528 | bytes 14155776 | tf_op jit(solution)/shard_map/dot_general | solution.py:66
  732.5 113.4 %all-reduce.8.cloned.1.call-done = f32[128,256]{1,0:T(8,128)} async-done(((f32[128,256]{1,0:T(8,128)}), f32[128,256]{1,0:T(8,128)}) %all-reduce.8.cloned.1.call-update) | async-done | bytes 131088 | tf_op jit(solution)/shard_map/psum | solution.py:30
  854.4 3.4 collective-permute-start.34
  859.1 14.7 %collective-permute-done.34 = f32[384,256]{0,1:T(8,128)S(1)} collective-permute-done((f32[384,256]{0,1:T(8,128)S(1)}, f32[384,256]{0,1:T(8,128)S(1)}, u32[]{:S(2)}, u32[]{:S(2)}) %collective-permute-start.34) | collective-permute-done | bytes 393248 | tf_op jit(solution)/shard_map/ppermute | solution.py:12
  876.9 17.9 %gather_fusion.10 = f32[1536,256]{1,0:T(8,128)} fusion(f32[4,384,256]{2,1,0:T(8,128)S(1)} %copy.41, s32[1536]{0:T(1024)S(1)} %reshape.175), kind=kCustom, calls=%fused_computation.10 | custom fusion | bytes 3158016 | tf_op jit(solution)/shard_map/gather | solution.py:24
  898.0 3.4 multiply_reduce_fusion
  901.4 43.2 %psum.47 = f32[256]{0:T(256)S(1)} all-reduce(f32[256]{0:T(256)S(1)} %get-tuple-element.12), channel_id=1, replica_groups=mesh['sx'=4,'sy'=8] {'sx','sy'}, use_global_device_ids=true, to_apply=%region_9.0 | all-reduce | flops 256 | bytes 2048 | tf_op jit(solution)/shard_map/psum | solution.py:76
  944.6 4.1 subtract_bitcast_fusion
  (149 shorter events, 108.9 us)
Async XLA Ops:
  7.2 274.2 %copy-start = (f32[1,1,16,1536]{3,2,1,0:T(8,128)S(1)}, f32[1,1,16,1536]{3,2,1,0:T(8,128)}, u32[]{:S(2)}) copy-start(f32[1,1,16,1536]{3,2,1,0:T(8,128)} %param.10) | copy-start | bytes 294916
  7.2 10.8 %copy-start.16 = (s32[1,1,4,384]{3,2,1,0:T(4,128)S(1)}, s32[1,1,4,384]{3,2,1,0:T(4,128)}, u32[]{:S(2)}) copy-start(s32[1,1,4,384]{3,2,1,0:T(4,128)} %param.12) | copy-start | bytes 18436
  7.2 397.1 %all-reduce.6.cloned.1.call-start = ((), (), s32[]{:S(2)}) async-start(), calls=%async_computation | async-start | bytes 262144 | tf_op jit(solution)/shard_map/psum | solution.py:30
  8.7 9.3 collective-permute-start
  11.1 6.9 collective-permute-start.1
  12.4 20.6 %collective-permute-start.2 = (f32[384,256]{1,0:T(8,128)S(1)}, f32[384,256]{1,0:T(8,128)S(1)}, u32[]{:S(2)}, u32[]{:S(2)}) collective-permute-start(f32[384,256]{1,0:T(8,128)S(1)} %get-tuple-element.50), channel_id=1, source_target_pairs={{0,1},{1,2},{2,3},{3,4},{4,5},{5,6},{6,7},{8,9},{9,10},{10,11},{11... | collective-permute-start | bytes 1179656 | tf_op jit(solution)/shard_map/ppermute | solution.py:12
  16.6 16.4 %collective-permute-start.3 = (f32[384,256]{1,0:T(8,128)S(1)}, f32[384,256]{1,0:T(8,128)S(1)}, u32[]{:S(2)}, u32[]{:S(2)}) collective-permute-start(f32[384,256]{1,0:T(8,128)S(1)} %get-tuple-element.52), channel_id=1, source_target_pairs={{1,0},{2,1},{3,2},{4,3},{5,4},{6,5},{7,6},{9,8},{10,9},{11,10},{12... | collective-permute-start | bytes 1179656 | tf_op jit(solution)/shard_map/ppermute | solution.py:12
  33.1 18.0 %copy-start.10 = (f32[1,1,1536,256]{3,2,1,0:T(8,128)S(1)}, f32[1,1,1536,256]{3,2,1,0:T(8,128)}, u32[]{:S(2)}) copy-start(f32[1,1,1536,256]{3,2,1,0:T(8,128)} %param.7) | copy-start | bytes 4718596
  54.1 10.3 %collective-permute-start.4 = (f32[384,256]{1,0:T(8,128)S(1)}, f32[384,256]{1,0:T(8,128)S(1)}, u32[]{:S(2)}, u32[]{:S(2)}) collective-permute-start(f32[384,256]{1,0:T(8,128)S(1)} %get-tuple-element.45), channel_id=1, source_target_pairs={{0,8},{8,16},{16,24},{1,9},{9,17},{17,25},{2,10},{10,18},{18,26},{... | collective-permute-start | bytes 1179656 | tf_op jit(solution)/shard_map/ppermute | solution.py:12
  57.7 6.7 collective-permute-start.5
  59.0 20.2 %collective-permute-start.6 = (f32[384,256]{1,0:T(8,128)S(1)}, f32[384,256]{1,0:T(8,128)S(1)}, u32[]{:S(2)}, u32[]{:S(2)}) collective-permute-start(f32[384,256]{1,0:T(8,128)S(1)} %get-tuple-element.47), channel_id=1, source_target_pairs={{0,1},{1,2},{2,3},{3,4},{4,5},{5,6},{6,7},{8,9},{9,10},{10,11},{11... | collective-permute-start | bytes 1179656 | tf_op jit(solution)/shard_map/ppermute | solution.py:12
  63.1 16.0 %collective-permute-start.7 = (f32[384,256]{1,0:T(8,128)S(1)}, f32[384,256]{1,0:T(8,128)S(1)}, u32[]{:S(2)}, u32[]{:S(2)}) collective-permute-start(f32[384,256]{1,0:T(8,128)S(1)} %get-tuple-element.46), channel_id=1, source_target_pairs={{1,0},{2,1},{3,2},{4,3},{5,4},{6,5},{7,6},{9,8},{10,9},{11,10},{12... | collective-permute-start | bytes 1179656 | tf_op jit(solution)/shard_map/ppermute | solution.py:12
  79.2 18.0 %copy-start.13 = (f32[4,384,256]{2,1,0:T(8,128)S(1)}, f32[4,384,256]{2,1,0:T(8,128)}, u32[]{:S(2)}) copy-start(f32[4,384,256]{2,1,0:T(8,128)} %copy-done.12) | copy-start | bytes 4718596
  117.3 10.9 %collective-permute-start.8 = (f32[384,256]{0,1:T(8,128)S(1)}, f32[384,256]{0,1:T(8,128)S(1)}, u32[]{:S(2)}, u32[]{:S(2)}) collective-permute-start(f32[384,256]{0,1:T(8,128)S(1)} %get-tuple-element.41), channel_id=1, source_target_pairs={{0,8},{8,16},{16,24},{1,9},{9,17},{17,25},{2,10},{10,18},{18,26},{... | collective-permute-start | bytes 1179656 | tf_op jit(solution)/shard_map/ppermute | solution.py:12
  121.2 7.0 collective-permute-start.9
  122.5 11.4 %collective-permute-start.10 = (f32[384,256]{0,1:T(8,128)S(1)}, f32[384,256]{0,1:T(8,128)S(1)}, u32[]{:S(2)}, u32[]{:S(2)}) collective-permute-start(f32[384,256]{0,1:T(8,128)S(1)} %get-tuple-element.43), channel_id=1, source_target_pairs={{0,1},{1,2},{2,3},{3,4},{4,5},{5,6},{6,7},{8,9},{9,10},{10,11},{11... | collective-permute-start | bytes 1179656 | tf_op jit(solution)/shard_map/ppermute | solution.py:12
  126.7 13.8 %collective-permute-start.11 = (f32[384,256]{0,1:T(8,128)S(1)}, f32[384,256]{0,1:T(8,128)S(1)}, u32[]{:S(2)}, u32[]{:S(2)}) collective-permute-start(f32[384,256]{0,1:T(8,128)S(1)} %get-tuple-element.42), channel_id=1, source_target_pairs={{1,0},{2,1},{3,2},{4,3},{5,4},{6,5},{7,6},{9,8},{10,9},{11,10},{12... | collective-permute-start | bytes 1179656 | tf_op jit(solution)/shard_map/ppermute | solution.py:12
  166.5 13.0 %copy-start.18 = (f32[4,128]{1,0:T(4,128)S(1)}, f32[4,128]{1,0:T(4,128)}, u32[]{:S(2)}) copy-start(f32[4,128]{1,0:T(4,128)} %param.13) | copy-start | bytes 6148
  166.5 91.8 %copy-start.17 = (s32[1,1,16]{2,1,0:T(1,128)S(1)}, s32[1,1,16]{2,1,0:T(1,128)}, u32[]{:S(2)}) copy-start(s32[1,1,16]{2,1,0:T(1,128)} %param.11) | copy-start | bytes 196
  166.6 91.7 %collective-permute-start.12 = (f32[384,256]{0,1:T(8,128)S(1)}, f32[384,256]{0,1:T(8,128)S(1)}, u32[]{:S(2)}, u32[]{:S(2)}) collective-permute-start(f32[384,256]{0,1:T(8,128)S(1)} %get-tuple-element.37), channel_id=1, source_target_pairs={{0,8},{8,16},{16,24},{1,9},{9,17},{17,25},{2,10},{10,18},{18,26},{... | collective-permute-start | bytes 1179656 | tf_op jit(solution)/shard_map/ppermute | solution.py:12
  172.8 85.6 %collective-permute-start.13 = (f32[384,256]{0,1:T(8,128)S(1)}, f32[384,256]{0,1:T(8,128)S(1)}, u32[]{:S(2)}, u32[]{:S(2)}) collective-permute-start(f32[384,256]{0,1:T(8,128)S(1)} %get-tuple-element.39), channel_id=1, source_target_pairs={{8,0},{16,8},{24,16},{9,1},{17,9},{25,17},{10,2},{18,10},{26,18},{... | collective-permute-start | bytes 1179656 | tf_op jit(solution)/shard_map/ppermute | solution.py:12
  174.1 84.3 %collective-permute-start.14 = (f32[384,256]{0,1:T(8,128)S(1)}, f32[384,256]{0,1:T(8,128)S(1)}, u32[]{:S(2)}, u32[]{:S(2)}) collective-permute-start(f32[384,256]{0,1:T(8,128)S(1)} %get-tuple-element.38), channel_id=1, source_target_pairs={{0,1},{1,2},{2,3},{3,4},{4,5},{5,6},{6,7},{8,9},{9,10},{10,11},{11... | collective-permute-start | bytes 1179656 | tf_op jit(solution)/shard_map/ppermute | solution.py:12
  178.2 80.2 %collective-permute-start.15 = (f32[384,256]{0,1:T(8,128)S(1)}, f32[384,256]{0,1:T(8,128)S(1)}, u32[]{:S(2)}, u32[]{:S(2)}) collective-permute-start(f32[384,256]{0,1:T(8,128)S(1)} %get-tuple-element.40), channel_id=1, source_target_pairs={{1,0},{2,1},{3,2},{4,3},{5,4},{6,5},{7,6},{9,8},{10,9},{11,10},{12... | collective-permute-start | bytes 1179656 | tf_op jit(solution)/shard_map/ppermute | solution.py:12
  283.7 562.3 %all-reduce.8.cloned.1.call-start = ((), (), s32[]{:S(2)}) async-start(), calls=%async_computation.1 | async-start | bytes 262144 | tf_op jit(solution)/shard_map/psum | solution.py:30
  409.0 20.8 %copy-start.11 = (f32[1,1,1536,256]{3,2,1,0:T(8,128)S(1)}, f32[1,1,1536,256]{3,2,1,0:T(8,128)}, u32[]{:S(2)}) copy-start(f32[1,1,1536,256]{3,2,1,0:T(8,128)} %param.7) | copy-start | bytes 4718596
  410.6 23.7 %collective-permute-start.16 = (f32[384,256]{0,1:T(8,128)}, f32[384,256]{0,1:T(8,128)}, u32[]{:S(2)}, u32[]{:S(2)}) collective-permute-start(f32[384,256]{0,1:T(8,128)} %get-tuple-element.33), channel_id=1, source_target_pairs={{0,8},{8,16},{16,24},{1,9},{9,17},{17,25},{2,10},{10,18},{18,26},{... | collective-permute-start | bytes 1179656 | tf_op jit(solution)/shard_map/ppermute | solution.py:12
  412.7 21.7 %collective-permute-start.17 = (f32[384,256]{0,1:T(8,128)}, f32[384,256]{0,1:T(8,128)}, u32[]{:S(2)}, u32[]{:S(2)}) collective-permute-start(f32[384,256]{0,1:T(8,128)} %get-tuple-element.36), channel_id=1, source_target_pairs={{8,0},{16,8},{24,16},{9,1},{17,9},{25,17},{10,2},{18,10},{26,18},{... | collective-permute-start | bytes 1179656 | tf_op jit(solution)/shard_map/ppermute | solution.py:12
  414.0 20.5 %collective-permute-start.18 = (f32[384,256]{0,1:T(8,128)}, f32[384,256]{0,1:T(8,128)}, u32[]{:S(2)}, u32[]{:S(2)}) collective-permute-start(f32[384,256]{0,1:T(8,128)} %get-tuple-element.35), channel_id=1, source_target_pairs={{0,1},{1,2},{2,3},{3,4},{4,5},{5,6},{6,7},{8,9},{9,10},{10,11},{11... | collective-permute-start | bytes 1179656 | tf_op jit(solution)/shard_map/ppermute | solution.py:12
  418.1 16.4 %collective-permute-start.19 = (f32[384,256]{0,1:T(8,128)}, f32[384,256]{0,1:T(8,128)}, u32[]{:S(2)}, u32[]{:S(2)}) collective-permute-start(f32[384,256]{0,1:T(8,128)} %get-tuple-element.34), channel_id=1, source_target_pairs={{1,0},{2,1},{3,2},{4,3},{5,4},{6,5},{7,6},{9,8},{10,9},{11,10},{12... | collective-permute-start | bytes 1179656 | tf_op jit(solution)/shard_map/ppermute | solution.py:12
  457.0 3.2 copy-start.9
  510.2 8.3 collective-permute-start.20
  511.5 7.0 collective-permute-start.21
  512.8 20.0 %collective-permute-start.22 = (f32[384,256]{0,1:T(8,128)S(1)}, f32[384,256]{0,1:T(8,128)S(1)}, u32[]{:S(2)}, u32[]{:S(2)}) collective-permute-start(f32[384,256]{0,1:T(8,128)S(1)} %get-tuple-element.31), channel_id=1, source_target_pairs={{0,1},{1,2},{2,3},{3,4},{4,5},{5,6},{6,7},{8,9},{9,10},{10,11},{11... | collective-permute-start | bytes 1179656 | tf_op jit(solution)/shard_map/ppermute | solution.py:12
  517.2 15.6 %collective-permute-start.23 = (f32[384,256]{0,1:T(8,128)S(1)}, f32[384,256]{0,1:T(8,128)S(1)}, u32[]{:S(2)}, u32[]{:S(2)}) collective-permute-start(f32[384,256]{0,1:T(8,128)S(1)} %get-tuple-element.30), channel_id=1, source_target_pairs={{1,0},{2,1},{3,2},{4,3},{5,4},{6,5},{7,6},{9,8},{10,9},{11,10},{12... | collective-permute-start | bytes 1179656 | tf_op jit(solution)/shard_map/ppermute | solution.py:12
  554.0 3.2 copy-start.5
  569.6 11.0 %collective-permute-start.24 = (f32[384,256]{0,1:T(8,128)S(1)}, f32[384,256]{0,1:T(8,128)S(1)}, u32[]{:S(2)}, u32[]{:S(2)}) collective-permute-start(f32[384,256]{0,1:T(8,128)S(1)} %get-tuple-element.25), channel_id=1, source_target_pairs={{0,8},{8,16},{16,24},{1,9},{9,17},{17,25},{2,10},{10,18},{18,26},{... | collective-permute-start | bytes 1179656 | tf_op jit(solution)/shard_map/ppermute | solution.py:12
  573.9 6.7 collective-permute-start.25
  575.2 19.4 %collective-permute-start.26 = (f32[384,256]{0,1:T(8,128)S(1)}, f32[384,256]{0,1:T(8,128)S(1)}, u32[]{:S(2)}, u32[]{:S(2)}) collective-permute-start(f32[384,256]{0,1:T(8,128)S(1)} %get-tuple-element.27), channel_id=1, source_target_pairs={{0,1},{1,2},{2,3},{3,4},{4,5},{5,6},{6,7},{8,9},{9,10},{10,11},{11... | collective-permute-start | bytes 1179656 | tf_op jit(solution)/shard_map/ppermute | solution.py:12
  579.3 15.3 %collective-permute-start.27 = (f32[384,256]{0,1:T(8,128)S(1)}, f32[384,256]{0,1:T(8,128)S(1)}, u32[]{:S(2)}, u32[]{:S(2)}) collective-permute-start(f32[384,256]{0,1:T(8,128)S(1)} %get-tuple-element.26), channel_id=1, source_target_pairs={{1,0},{2,1},{3,2},{4,3},{5,4},{6,5},{7,6},{9,8},{10,9},{11,10},{12... | collective-permute-start | bytes 1179656 | tf_op jit(solution)/shard_map/ppermute | solution.py:12
  669.7 8.5 collective-permute-start.28
  671.0 7.2 collective-permute-start.29
  672.3 20.0 %collective-permute-start.30 = (f32[384,256]{0,1:T(8,128)S(1)}, f32[384,256]{0,1:T(8,128)S(1)}, u32[]{:S(2)}, u32[]{:S(2)}) collective-permute-start(f32[384,256]{0,1:T(8,128)S(1)} %get-tuple-element.23), channel_id=1, source_target_pairs={{0,1},{1,2},{2,3},{3,4},{4,5},{5,6},{6,7},{8,9},{9,10},{10,11},{11... | collective-permute-start | bytes 1179656 | tf_op jit(solution)/shard_map/ppermute | solution.py:12
  676.7 15.6 %collective-permute-start.31 = (f32[384,256]{0,1:T(8,128)S(1)}, f32[384,256]{0,1:T(8,128)S(1)}, u32[]{:S(2)}, u32[]{:S(2)}) collective-permute-start(f32[384,256]{0,1:T(8,128)S(1)} %get-tuple-element.22), channel_id=1, source_target_pairs={{1,0},{2,1},{3,2},{4,3},{5,4},{6,5},{7,6},{9,8},{10,9},{11,10},{12... | collective-permute-start | bytes 1179656 | tf_op jit(solution)/shard_map/ppermute | solution.py:12
  713.4 3.2 copy-start.2
  851.8 7.3 collective-permute-start.32
  853.1 6.0 collective-permute-start.33
  854.4 19.4 %collective-permute-start.34 = (f32[384,256]{0,1:T(8,128)S(1)}, f32[384,256]{0,1:T(8,128)S(1)}, u32[]{:S(2)}, u32[]{:S(2)}) collective-permute-start(f32[384,256]{0,1:T(8,128)S(1)} %get-tuple-element.19), channel_id=1, source_target_pairs={{0,1},{1,2},{2,3},{3,4},{4,5},{5,6},{6,7},{8,9},{9,10},{10,11},{11... | collective-permute-start | bytes 1179656 | tf_op jit(solution)/shard_map/ppermute | solution.py:12
  857.8 16.0 %collective-permute-start.35 = (f32[384,256]{0,1:T(8,128)S(1)}, f32[384,256]{0,1:T(8,128)S(1)}, u32[]{:S(2)}, u32[]{:S(2)}) collective-permute-start(f32[384,256]{0,1:T(8,128)S(1)} %get-tuple-element.18), channel_id=1, source_target_pairs={{1,0},{2,1},{3,2},{4,3},{5,4},{6,5},{7,6},{9,8},{10,9},{11,10},{12... | collective-permute-start | bytes 1179656 | tf_op jit(solution)/shard_map/ppermute | solution.py:12
  (9 other events, 16.9 us)
Sparse Core Ops, SparseCore 0:
  283.8 120.4 all-reduce.5
  720.4 125.4 all-reduce.7
where the time goes:
time: 971 us; the launch traced here: 961 us
  waiting for transfers between devices  322 us (33%)
  local copies, waits for them, and re-layouts  216 us (22%)
  blocking collectives  210 us (22%)
  starting transfers between devices  97.3 us (10%)
  matrix products  67.2 us (7%)
  other arithmetic  34.3 us (4%)
  between operations  15.2 us (2%)
    psum x2, waiting for transfers between devices, coarse_solve(): total = lax.psum(coarse_rhs, ('sx', 'sy'))  222 us
    gather x17, local copies, waits for them, and re-layouts, jump(): matched = received[jnp.arange(4, dtype=jnp.int32)[:, None], face_index]  186 us
    ppermute x36, waiting for transfers between devices, shifted(): return lax.ppermute(block, axis, route)  99.1 us
    ppermute x36, starting transfers between devices, shifted(): return lax.ppermute(block, axis, route)  97.3 us
    psum x2, blocking collectives, residual_dot(): return lax.psum(inner(residual, precond), ('sx', 'sy'))  87.5 us
    all_gather x1, blocking collectives, shards(): lax.all_gather(coarse_inverse, ('sx', 'sy'), axis=0, tiled=True)  78.8 us
    psum x1, blocking collectives, shards(): lax.psum(inner(direction, image_dir), ('sx', 'sy'))  43.2 us
    dot_general x2, matrix products, precondition(): operator_applied = jnp.dot(prec_mat, spread, precision=highest)  29.5 us
  transfers between devices with their start and end apart: 38, of which 11 were waited for; matrix products, arithmetic and copies ran while one was open for 3% of the time, Pallas kernels for 0%

commit v1 on v0

v1 whole, which is shorter than its diff:
```python
import functools

import jax
import jax.numpy as jnp
from jax import lax
from jax.experimental import pallas as pl
from jax.experimental.pallas import tpu as pltpu
from jax.sharding import PartitionSpec as P

HIGHEST = lax.Precision.HIGHEST
HIGH = lax.Precision.HIGH
F32 = jnp.float32
BF16 = jnp.bfloat16
LIMIT = 40 * 1024 * 1024


def shifted(block, axis, distance):
    devices = range(lax.axis_size(axis))
    route = [(i - distance, i) for i in devices if i - distance in devices]
    return lax.ppermute(block, axis, route)


def facing(low, high, axis):
    return shifted(high, axis, 1), shifted(low, axis, -1)


def from_all(rows):
    count = lax.axis_size("sx") * lax.axis_size("sy")
    copies = jnp.broadcast_to(rows[None], (count,) + rows.shape)
    return lax.all_to_all(copies, ("sx", "sy"), 0, 0, tiled=True)


def split(x):
    high = x.astype(BF16)
    return high, (x - high.astype(F32)).astype(BF16)


def dot(a, b):
    return jnp.dot(a, b, preferred_element_type=F32)


def product(a, b_high, b_low):
    a_high, a_low = split(a)
    return dot(a_high, b_high) + (dot(a_high, b_low) + dot(a_low, b_high))


def permuted(select, rows):
    high = rows.astype(BF16)
    rest = rows - high.astype(F32)
    mid = rest.astype(BF16)
    low = (rest - mid.astype(F32)).astype(BF16)
    return dot(select, high) + (dot(select, mid) + dot(select, low))


def spread_into(at, refs, select, scale, coef, bases, outs, high, low):
    owns, nears = refs
    size = owns[0].shape[0]
    for f in range(2):
        value = coef[...] * (owns[f][...] - permuted(select[f], nears[f][:size]))
        if bases:
            value = bases[f][...] + value
        outs[f][...] = value
        high[f * size : (f + 1) * size], low[f * size : (f + 1) * size] = split(scale[at + f] * value)


def early_kernel(based, *refs):
    scale, mat, own0, own1, near0, near1, select, coef = refs[:8]
    bases, (out0, out1, partial, high, low) = refs[8 : 8 + 2 * based], refs[8 + 2 * based :]

    @pl.when(pl.program_id(0) == 0)
    def _():
        spread_into(0, ((own0, own1), (near0, near1)), select, scale, coef, bases, (out0, out1), high, low)

    partial[...] = product(mat[...], high[...], low[...])


def crit_kernel(based, extended, *refs):
    scale, mat, own2, own3, near2, near3, select, coef, partial = refs[:9]
    rest = refs[9:]
    bases, rest = rest[: 2 * based], rest[2 * based :]
    extra, rest = rest[:extended], rest[extended:]
    out2, out3, applied2, applied3, high, low = rest

    @pl.when(pl.program_id(0) == 0)
    def _():
        spread_into(2, ((own2, own3), (near2, near3)), select, scale, coef, bases, (out2, out3), high, low)

    value = partial[...] + product(mat[...], high[...], low[...])
    if extended:
        value = value + extra[0][...]
    for at, ref in enumerate((applied2, applied3)):

        @pl.when(pl.program_id(0) == at)
        def _(ref=ref):
            ref[...] = value


def late_kernel(extended, *refs):
    scale, mat, value2, value3, partial = refs[:5]
    extra, rest = refs[5 : 5 + extended], refs[5 + extended :]
    applied0, applied1, high, low = rest
    size = value2.shape[0]

    @pl.when(pl.program_id(0) == 0)
    def _():
        for f, ref in enumerate((value2, value3)):
            high[f * size : (f + 1) * size], low[f * size : (f + 1) * size] = split(scale[2 + f] * ref[...])

    value = partial[...] + product(mat[...], high[...], low[...])
    if extended:
        value = value + extra[0][...]
    for at, ref in enumerate((applied0, applied1)):

        @pl.when(pl.program_id(0) == at)
        def _(ref=ref):
            ref[...] = value


def tail_kernel(*refs):
    owns, nears, bases = refs[:4], refs[4:8], refs[8:12]
    select, coef, out = refs[12:]
    size = out.shape[0]
    for f in range(4):

        @pl.when(pl.program_id(0) == f)
        def _(f=f):
            out[...] = bases[f][...] + coef[...] * (owns[f][...] - permuted(select[0], nears[f][:size]))


def weighted_kernel(*refs):
    firsts, seconds = refs[:4], refs[4:8]
    first_coef, second_coef, out = refs[8:]
    for f in range(4):

        @pl.when(pl.program_id(0) == f)
        def _(f=f):
            out[...] = first_coef[...] * firsts[f][...] + second_coef[...] * seconds[f][...]


def whole(array):
    return pl.BlockSpec(array.shape, lambda i, n=array.ndim: (0,) * n)


def call(kernel, grid, operands, outs, scratch, flops):
    arrays = [a for a, _ in operands]
    moved = sum(a.size * a.dtype.itemsize for a in arrays)
    return pl.pallas_call(
        kernel,
        grid=(grid,),
        in_specs=[s for _, s in operands],
        out_specs=[s for _, s in outs],
        out_shape=[jax.ShapeDtypeStruct(s, F32) for s, _ in outs],
        scratch_shapes=scratch,
        compiler_params=pltpu.CompilerParams(vmem_limit_bytes=LIMIT),
        cost_estimate=pl.CostEstimate(flops=flops, bytes_accessed=moved, transcendentals=0),
    )(*arrays)


def shards(loads, schur_flex, dirichlet, coupling, corner_index, face_lists, coarse_inverse):
    flex_mat = schur_flex[0, 0]
    prec_mat = dirichlet[0, 0]
    coupling_mat = coupling[0, 0]
    corners = corner_index[0, 0]
    face_index = face_lists[0, 0]
    load = loads[0, 0]
    ncoarse = coarse_inverse.shape[1]
    ncl, ni = coupling_mat.shape
    width = load.shape[1]
    face, half = ni // 4, ni // 2
    n_sx, n_sy = lax.axis_size("sx"), lax.axis_size("sy")
    at_x, at_y = lax.axis_index("sx"), lax.axis_index("sy")

    has = jnp.stack([at_x > 0, at_x < n_sx - 1, at_y > 0, at_y < n_sy - 1])
    scale = jnp.where(has, 2.0, 1.0).astype(F32)
    select = (face_index[:, :, None] == jnp.arange(face, dtype=jnp.int32)).astype(BF16)
    one = jnp.ones((1, width), F32)
    smem = pl.BlockSpec(memory_space=pltpu.SMEM)

    one_face = jax.ShapeDtypeStruct((face, width), F32)
    face_out = ((face, width), whole(one_face))
    parts = [pltpu.VMEM((half, width), BF16), pltpu.VMEM((half, width), BF16)]
    part_flops = 6 * half * half * width

    def exchange_y(faces):
        return facing(faces[2], faces[3], "sy")

    def exchange_x(faces):
        return facing(faces[0], faces[1], "sx")

    def with_whole(arrays):
        return [(a, whole(a)) for a in arrays]

    def early(matrix, owns, nears, coef, bases=()):
        operands = [(scale, smem), (matrix, pl.BlockSpec((face, half), lambda i: (i, 0)))]
        operands += with_whole([*owns, *nears])
        operands += [(select, pl.BlockSpec((2, face, face), lambda i: (0, 0, 0))), (coef, whole(coef))]
        operands += with_whole(bases)
        outs = [face_out, face_out, ((ni, width), pl.BlockSpec((face, width), lambda i: (i, 0)))]
        return call(functools.partial(early_kernel, bool(bases)), 4, operands, outs, parts, 2 * part_flops)

    def crit(matrix, owns, nears, coef, partial, bases=(), extra=()):
        operands = [(scale, smem), (matrix, pl.BlockSpec((face, half), lambda i: (i + 2, 1)))]
        operands += with_whole([*owns, *nears])
        operands += [(select, pl.BlockSpec((2, face, face), lambda i: (1, 0, 0))), (coef, whole(coef))]
        operands += [(partial, pl.BlockSpec((face, width), lambda i: (i + 2, 0)))]
        operands += with_whole(bases)
        operands += [(a, pl.BlockSpec((face, width), lambda i: (i + 2, 0))) for a in extra]
        kernel = functools.partial(crit_kernel, bool(bases), len(extra))
        return call(kernel, 2, operands, [face_out] * 4, parts, part_flops)

    def late(matrix, values, partial, extra=()):
        operands = [(scale, smem), (matrix, pl.BlockSpec((face, half), lambda i: (i, 1)))]
        operands += with_whole(values)
        operands += [(partial, pl.BlockSpec((face, width), lambda i: (i, 0)))]
        operands += [(a, pl.BlockSpec((face, width), lambda i: (i, 0))) for a in extra]
        return call(functools.partial(late_kernel, len(extra)), 2, operands, [face_out] * 2, parts, part_flops)

    def applied(matrix, owns, nears, coef, bases=(), extra=()):
        v0, v1, partial = early(matrix, owns[:2], nears[:2], coef, bases[:2])
        v2, v3, a2, a3 = crit(matrix, owns[2:], nears[2:], coef, partial, bases[2:], extra)
        a0, a1 = late(matrix, (v2, v3), partial, extra)
        return (v0, v1, v2, v3), (a0, a1, a2, a3)

    def exchanged(faces):
        far = exchange_y(faces)
        return (*exchange_x(faces), *far)

    def inner(first, second):
        return sum(jnp.sum(scale[f] * first[f] * second[f], axis=0, keepdims=True) for f in range(4))

    def rows_of(array):
        return [array[f * face : (f + 1) * face] for f in range(4)]

    load_faces = rows_of(load)
    sent = []
    for f in range(4):
        columns = jnp.pad(coupling_mat[:, f * face : (f + 1) * face], ((0, 0), (0, -face % width)))
        blocks = [columns[:, at : at + width] for at in range(0, columns.shape[1], width)]
        sent.append(jnp.concatenate([load_faces[f], *blocks], axis=0))
    near = exchanged(sent)

    listed = jnp.zeros((1, ncoarse), F32).at[0, :ncl].set(corners.astype(F32))
    table = from_all(jnp.concatenate([coarse_inverse, listed], axis=0))
    matrix_all = table[:, :-1].reshape(ncoarse, ncoarse)
    corners_all = table[:, -1, :ncl].astype(jnp.int32)
    coarse_ids = jnp.arange(ncoarse, dtype=jnp.int32)[:, None]

    me = at_x * n_sy + at_y
    there = [me - n_sy, me + n_sy, me - 1, me + 1]
    lift = []
    for f in range(4):
        columns = jnp.concatenate(
            [near[f][at : at + ncl] for at in range(face, near[f].shape[0], ncl)], axis=1
        )[:, :face]
        theirs = lax.dot_general(columns, select[f].astype(F32), (((1,), (1,)), ((), ())), precision=HIGHEST)
        ids = jnp.concatenate([corners, corners_all[jnp.clip(there[f], 0, n_sx * n_sy - 1)]])
        values = jnp.concatenate([coupling_mat[:, f * face : (f + 1) * face], -theirs], axis=0)
        lift.append(jnp.dot((coarse_ids == ids[None, :]).astype(F32), values, precision=HIGHEST))
    lift = jnp.concatenate(lift, axis=1)
    lift_spread = lift * jnp.repeat(scale, face)[None, :]

    def coarse_sum(faces):
        local = sum(
            jnp.dot(lift_spread[:, f * face : (f + 1) * face], faces[f], precision=HIGH) for f in range(4)
        )
        return lax.psum(lax.psum(0.5 * local, "sx"), "sy")

    def lifted(sol):
        full = lax.dot_general(lift, sol, (((0,), (0,)), ((), ())), precision=HIGH)
        return rows_of(full)

    def dots_sum(dots):
        return jnp.sum(from_all(jnp.concatenate(dots, axis=0)), axis=0)

    residual0, applied0 = applied(prec_mat, load_faces, near, one)
    near = exchanged(applied0)
    rho0 = 0.5 * inner(residual0, applied0)
    rhs0 = coarse_sum(applied0)
    lift_applied = lax.dot_general(prec_mat, lift_spread, (((1,), (1,)), ((), ())), precision=HIGH)

    direction0, fine0 = applied(flex_mat, applied0, near, 0.5 * one)
    near = exchanged(fine0)
    dots0 = dots_sum([rho0, inner(direction0, fine0)])
    sol0 = jnp.dot(matrix_all, rhs0, precision=HIGHEST)
    lift_sol = jnp.dot(lift_applied, sol0, precision=HIGH)
    jump0, image_applied = applied(prec_mat, fine0, near, one, (), (lift_sol,))
    near = exchanged(image_applied)
    rho0, fine_dot0 = dots0[0:1], dots0[1:2]
    step0 = rho0 / (fine_dot0 + jnp.sum(rhs0 * sol0, axis=0, keepdims=True))
    rhs1 = rhs0 - step0 * coarse_sum(image_applied)
    lift0 = lifted(sol0)
    residual1 = [r - step0 * (j + c) for r, j, c in zip(residual0, jump0, lift0)]
    applied1 = [z - step0 * y for z, y in zip(applied0, image_applied)]
    rho1 = 0.5 * inner(residual1, applied1)

    precond, fine1 = applied(flex_mat, image_applied, near, -0.5 * step0, direction0)
    near = exchanged(fine1)
    dots1 = dots_sum([rho1, inner(precond, fine1), inner(precond, fine0)])
    rho1, dot11, dot10 = dots1[0:1], dots1[1:2], dots1[2:3]
    beta = rho1 / rho0
    rhs1 = rhs1 + beta * rhs0
    sol1 = jnp.dot(matrix_all, rhs1, precision=HIGHEST)
    curve = dot11 + 2.0 * beta * dot10 + beta * beta * fine_dot0 + jnp.sum(rhs1 * sol1, axis=0, keepdims=True)
    step1 = rho1 / curve
    lift1 = lifted(sol1)
    bases = [r - step1 * (beta * j + c) for r, j, c in zip(residual1, jump0, lift1)]
    block = pl.BlockSpec((face, width), lambda i: (i, 0))
    (multipliers,) = call(
        weighted_kernel,
        4,
        with_whole([*direction0, *precond, step0 + step1 * beta, step1]),
        [((ni, width), block)],
        [],
        4 * ni * width,
    )
    operands = with_whole([*fine1, *near, *bases])
    operands += [(select, pl.BlockSpec((1, face, face), lambda i: (i, 0, 0)))] + with_whole([-step1])
    (residual2,) = call(tail_kernel, 4, operands, [((ni, width), block)], [], 6 * ni * face * width)
    return multipliers[None, None], residual2[None, None]


def solution(mesh):
    return jax.shard_map(
        shards,
        mesh=mesh,
        in_specs=(
            P("sx", "sy", None, None),
            P("sx", "sy", None, None),
            P("sx", "sy", None, None),
            P("sx", "sy", None, None),
            P("sx", "sy", None),
            P("sx", "sy", None, None),
            P(("sx", "sy"), None),
        ),
        out_specs=(P("sx", "sy", None, None), P("sx", "sy", None, None)),
        check_vma=False,
    )
```

time: 971 us -> 441 us (0.45)
  blocking collectives: 210 us -> 0 us
  local copies, waits for them, and re-layouts: 216 us -> 19.3 us
  waiting for transfers between devices: 322 us -> 217 us
  Pallas kernels: 0 us -> 54.8 us
  matrix products: 67.2 us -> 33.7 us
  starting transfers between devices: 97.3 us -> 68.3 us
    gather x19 -> x0, local copies, waits for them, and re-layouts: 187 us -> none  [the longest x17 186 us: jump(): matched = received[jnp.arange(4, dtype=jnp.int32)[:, None], face_index]]
    psum x3 -> x0, blocking collectives: 131 us -> none  [the longest x2 87.5 us: residual_dot(): return lax.psum(inner(residual, precond), ('sx', 'sy'))]
    ppermute x36 -> x20, waiting for transfers between devices: 99.1 us -> 14 us  [shifted(): return lax.ppermute(block, axis, route)]
    all_gather x1 -> x0, blocking collectives: 78.8 us -> none  [shards(): lax.all_gather(coarse_inverse, ('sx', 'sy'), axis=0, tiled=True)]
    pallas_call x0 -> x14, Pallas kernels: none -> 54.8 us  [call(): pl.pallas_call(kernel, grid=(grid,), in_specs=[s for _, s in operands], o...]
    ppermute x36 -> x20, starting transfers between devices: 97.3 us -> 44.5 us  [shifted(): return lax.ppermute(block, axis, route)]
    dot_general x12 -> x22, matrix products: 67.2 us -> 33.7 us  [the longest x1 9.62 us: shards(): lax.dot_general(prec_mat, lift_spread, (((1,), (1,)), ((), ())), precisio...]
    all_to_all x0 -> x3, starting transfers between devices: none -> 23.5 us  [from_all(): return lax.all_to_all(copies, ('sx', 'sy'), 0, 0, tiled=True)]
  transfers between devices with their start and end apart: 38 -> 27, of which waited for: 11 -> 7; matrix products, arithmetic and copies ran while one was open for 3% -> 12% of each run, Pallas kernels for 0% -> 4%
where the time goes in v1:
time: 441 us; the launch traced here: 439 us
  waiting for transfers between devices  217 us (49%)
  starting transfers between devices  68.3 us (15%)
  Pallas kernels  54.8 us (12%)
  matrix products  33.7 us (8%)
  other arithmetic  30.8 us (7%)
  local copies, waits for them, and re-layouts  19.3 us (4%)
  between operations  15.3 us (3%)
    psum x4, waiting for transfers between devices, coarse_sum(): return lax.psum(lax.psum(0.5 * local, 'sx'), 'sy')  202 us
    pallas_call x14, Pallas kernels, call(): pl.pallas_call(kernel, grid=(grid,), in_specs=[s for _, s in operands], o...  54.8 us
    ppermute x20, starting transfers between devices, shifted(): return lax.ppermute(block, axis, route)  44.5 us
    all_to_all x3, starting transfers between devices, from_all(): return lax.all_to_all(copies, ('sx', 'sy'), 0, 0, tiled=True)  23.5 us
    reduce_sum x10, other arithmetic, inner(): jnp.sum(scale[f] * first[f] * second[f], axis=0, keepdims=True)  18.8 us
    ppermute x20, waiting for transfers between devices, shifted(): return lax.ppermute(block, axis, route)  14 us
    unnamed x164, local copies, waits for them, and re-layouts  10.5 us
    dot_general x1, matrix products, shards(): lax.dot_general(prec_mat, lift_spread, (((1,), (1,)), ((), ())), precisio...  9.62 us
  transfers between devices with their start and end apart: 27, of which 7 were waited for; matrix products, arithmetic and copies ran while one was open for 12% of the time, Pallas kernels for 4%

profile of v1, /device:TPU:0, one launch (start us, length us, event | category | flops | bytes accessed | tf_op | source)
XLA Modules:
  0.0 438.7 jit_solution(3077997246190898142)
XLA Ops:
  10.4 7.3 %all-to-all-start = ((f32[32,5,128]{2,1,0:T(8,128)}), f32[32,5,128]{2,1,0:T(8,128)S(1)}, u32[]{:S(2)}, u32[]{:S(2)}) async-start(f32[32,5,128]{2,1,0:T(8,128)} %broadcast_in_dim.29), calls=%async_computation | async-start | bytes 262144 | tf_op jit(solution)/shard_map/all_to_all | solution.py:30
  19.4 1.5 slice_bitcast_fusion.8
  21.7 3.8 collective-permute-start
  28.4 2.7 collective-permute-start.2
  36.8 7.4 %collective-permute-done.refs_4_ = f32[416,256]{1,0:T(8,128)S(1)} collective-permute-done((f32[416,256]{1,0:T(8,128)}, f32[416,256]{1,0:T(8,128)S(1)}, u32[]{:S(2)}, u32[]{:S(2)}) %collective-permute-start) | collective-permute-done | bytes 426016 | tf_op jit(solution)/shard_map/ppermute | solution.py:20
  52.7 9.6 %fusion.77 = f32[128,1536]{1,0:T(8,128)} fusion(f32[128,1536]{1,0:T(8,128)S(1)} %broadcast_multiply_fusion, f32[1,1,1536,1536]{3,2,1,0:T(8,128)} %param.11), kind=kOutput, calls=%fused_computation.170 | convolution fusion | flops 1811939328 | bytes 11010048 | tf_op jit(solution)/shard_map/dot_general | solution.py:279
  62.4 6.2 %shard_map.86 = (f32[384,256]{1,0:T(8,128)S(1)}, f32[384,256]{1,0:T(8,128)S(1)}, f32[1536,256]{1,0:T(8,128)S(1)}) custom-call(f32[4]{0:T(128)S(1)} %add_select_fusion.refs_0_, f32[1536,1536]{1,0:T(8,128)} %bitcast.74, f32[384,256]{1,0:T(8,128)S(1)} %get-tuple-element.108.refs_2_, f32[384,256]{1,0:T(8,128)S(1)} %get-tuple-element.105.refs_3_, ...), custom_call_target="tpu_custom_call" | custom-call | flops 1811939328 | bytes 12256272 | tf_op jit(solution)/shard_map/pallas_call | solution.py:147
  68.7 3.8 shard_map.87
  72.6 3.0 shard_map.88
  76.9 2.0 collective-permute-start.4
  79.2 5.0 %collective-permute-start.6 = (f32[384,256]{1,0:T(8,128)S(1)}, f32[384,256]{1,0:T(8,128)}, u32[]{:S(2)}, u32[]{:S(2)}) collective-permute-start(f32[384,256]{1,0:T(8,128)S(1)} %get-tuple-element.58.refs_3_), channel_id=1, source_target_pairs={{0,1},{1,2},{2,3},{3,4},{4,5},{5,6},{6,7},{8,9},{9,10},{10,11},{11... | collective-permute-start | bytes 1179656 | tf_op jit(solution)/shard_map/ppermute | solution.py:20
  89.4 2.0 multiply_reduce_fusion.16
  91.4 3.2 multiply_reduce_fusion.18
  94.6 29.1 %all-reduce.9.cloned.1.call-done = f32[128,256]{1,0:T(8,128)} async-done(((f32[128,256]{1,0:T(8,128)}), f32[128,256]{1,0:T(8,128)}) %all-reduce.9.cloned.1.call-update) | async-done | bytes 131088 | tf_op jit(solution)/shard_map/psum | solution.py:266
  124.4 72.8 %all-reduce.11.cloned.1.call-done = f32[128,256]{1,0:T(8,128)} async-done(((f32[128,256]{1,0:T(8,128)}), f32[128,256]{1,0:T(8,128)}) %all-reduce.11.cloned.1.call-update) | async-done | bytes 131088 | tf_op jit(solution)/shard_map/psum | solution.py:266
  197.2 1.8 multiply_reduce_fusion.21
  199.0 2.0 fusion.88.refs_9_.refs_5_
  201.0 3.7 copy-done.1
  204.6 5.4 %shard_map.89 = (f32[384,256]{1,0:T(8,128)S(1)}, f32[384,256]{1,0:T(8,128)S(1)}, f32[1536,256]{1,0:T(8,128)S(1)}) custom-call(f32[4]{0:T(128)S(1)} %add_select_fusion.refs_0_, f32[1536,1536]{1,0:T(8,128)S(1)} %bitcast.87, f32[384,256]{1,0:T(8,128)} %get-tuple-element.53.refs_2_, f32[384,256]{1,0:T(8,128)} %get-tuple-element.54.refs_3_, ...), custom_call_target="tpu_custom_call" | custom-call | flops 1811939328 | bytes 12190736 | tf_op jit(solution)/shard_map/pallas_call | solution.py:147
  210.1 5.0 %shard_map.90 = (f32[384,256]{1,0:T(8,128)S(1)}, f32[384,256]{1,0:T(8,128)S(1)}, f32[384,256]{1,0:T(8,128)}, f32[384,256]{1,0:T(8,128)}) custom-call(f32[4]{0:T(128)S(1)} %add_select_fusion.refs_0_, f32[1536,1536]{1,0:T(8,128)} %bitcast.84, f32[384,256]{1,0:T(8,128)S(1)} %get-tuple-element.57.refs_2_, f32[384,256]{1,0:T(8,128)S(1)} %get-tuple-element.58.refs_3_, ...), custom_call_target="tpu_custom_call" | custom-call | flops 905969664 | bytes 13763600 | tf_op jit(solution)/shard_map/pallas_call | solution.py:147
  215.1 2.1 shard_map.91
  221.4 2.6 multiply_reduce_fusion.12
  224.6 7.0 %all-to-all-start.1 = ((f32[32,2,256]{2,1,0:T(2,128)}), f32[32,2,256]{2,1,0:T(2,128)}, u32[]{:S(2)}, u32[]{:S(2)}) async-start(f32[32,2,256]{2,1,0:T(2,128)} %broadcast_in_dim.31), calls=%async_computation.1 | async-start | bytes 131072 | tf_op jit(solution)/shard_map/all_to_all | solution.py:30
  231.6 3.1 fusion.33
  234.7 4.3 collective-permute-start.8
  241.9 3.7 copy-done
  245.6 5.0 %shard_map.92 = (f32[384,256]{1,0:T(8,128)S(1)}, f32[384,256]{1,0:T(8,128)S(1)}, f32[1536,256]{1,0:T(8,128)S(1)}) custom-call(f32[4]{0:T(128)S(1)} %add_select_fusion.refs_0_, f32[1536,1536]{1,0:T(8,128)S(1)} %bitcast.80, f32[384,256]{1,0:T(8,128)S(1)} %get-tuple-element.64.refs_2_, f32[384,256]{1,0:T(8,128)S(1)} %get-tuple-element.65.refs_3_, ...), custom_call_target="tpu_custom_call" | custom-call | flops 1811939328 | bytes 12190736 | tf_op jit(solution)/shard_map/pallas_call | solution.py:147
  250.5 5.1 %collective-permute-done.8.refs_4_ = f32[384,256]{1,0:T(8,128)} collective-permute-done((f32[384,256]{1,0:T(8,128)}, f32[384,256]{1,0:T(8,128)}, u32[]{:S(2)}, u32[]{:S(2)}) %collective-permute-start.8) | collective-permute-done | bytes 393248 | tf_op jit(solution)/shard_map/ppermute | solution.py:20
  257.1 4.2 shard_map.93
  261.4 2.1 shard_map.94
  266.2 4.4 %collective-permute-start.14 = (f32[384,256]{1,0:T(8,128)S(1)}, f32[384,256]{1,0:T(8,128)S(1)}, u32[]{:S(2)}, u32[]{:S(2)}) collective-permute-start(f32[384,256]{1,0:T(8,128)S(1)} %get-tuple-element.76.refs_3_), channel_id=1, source_target_pairs={{0,1},{1,2},{2,3},{3,4},{4,5},{5,6},{6,7},{8,9},{9,10},{10,11},{11... | collective-permute-start | bytes 1179656 | tf_op jit(solution)/shard_map/ppermute | solution.py:20
  272.8 1.5 collective-permute-start.15
  274.4 3.5 multiply_reduce_fusion.10
  279.0 6.0 %shard_map.95 = (f32[384,256]{1,0:T(8,128)S(1)}, f32[384,256]{1,0:T(8,128)S(1)}, f32[1536,256]{1,0:T(8,128)S(1)}) custom-call(f32[4]{0:T(128)S(1)} %add_select_fusion.refs_0_, f32[1536,1536]{1,0:T(8,128)} %bitcast.85, f32[384,256]{1,0:T(8,128)S(1)} %get-tuple-element.69.refs_2_, f32[384,256]{1,0:T(8,128)S(1)} %get-tuple-element.70.refs_3_, ...), custom_call_target="tpu_custom_call" | custom-call | flops 1811939328 | bytes 12977168 | tf_op jit(solution)/shard_map/pallas_call | solution.py:147
  286.4 3.7 shard_map.96
  290.2 2.1 shard_map.97
  292.4 1.8 multiply_reduce_fusion.5
  294.2 1.8 multiply_reduce_fusion.4
  298.3 9.2 %all-to-all-start.2 = ((f32[32,3,256]{2,1,0:T(4,128)}), f32[32,3,256]{2,1,0:T(4,128)}, u32[]{:S(2)}, u32[]{:S(2)}) async-start(f32[32,3,256]{2,1,0:T(4,128)} %broadcast_in_dim.33), calls=%async_computation.2 | async-start | bytes 262144 | tf_op jit(solution)/shard_map/all_to_all | solution.py:30
  307.6 2.1 fusion.1
  309.7 33.5 %all-reduce.13.cloned.1.call-done = f32[128,256]{1,0:T(8,128)} async-done(((f32[128,256]{1,0:T(8,128)}), f32[128,256]{1,0:T(8,128)}) %all-reduce.13.cloned.1.call-update) | async-done | bytes 131088 | tf_op jit(solution)/shard_map/psum | solution.py:266
  343.3 2.1 collective-permute-start.16
  346.6 4.2 collective-permute-start.18
  353.1 67.0 %all-reduce.15.cloned.1.call-done = f32[128,256]{1,0:T(8,128)} async-done(((f32[128,256]{1,0:T(8,128)}), f32[128,256]{1,0:T(8,128)}) %all-reduce.15.cloned.1.call-update) | async-done | bytes 131088 | tf_op jit(solution)/shard_map/psum | solution.py:266
  420.1 1.6 multiply_reduce_fusion.20
  421.7 2.0 fusion.32
  423.9 1.8 shard_map.98
  427.7 4.4 %shard_map.99 = f32[1536,256]{1,0:T(8,128)} custom-call(f32[384,256]{1,0:T(8,128)S(1)} %copy-done.46, f32[384,256]{1,0:T(8,128)S(1)} %copy-done.48, f32[384,256]{1,0:T(8,128)S(1)} %copy-done.42, f32[384,256]{1,0:T(8,128)S(1)} %copy-done.44, f32[384,256]{1,0:T(8,128)} %collective-permute-done.16.refs_4_, f32[384,256]{1,0:T(8,128)} %collective-permute-done.17.refs_5_, ...), custom_call_target="tpu_custom_call" | custom-call | flops 905969664 | bytes 5899264 | tf_op jit(solution)/shard_map/pallas_call | solution.py:147
  (272 shorter events, 54.2 us)
Async XLA Ops:
  10.4 25.6 %all-to-all-start = ((f32[32,5,128]{2,1,0:T(8,128)}), f32[32,5,128]{2,1,0:T(8,128)S(1)}, u32[]{:S(2)}, u32[]{:S(2)}) async-start(f32[32,5,128]{2,1,0:T(8,128)} %broadcast_in_dim.29), calls=%async_computation | async-start | bytes 262144 | tf_op jit(solution)/shard_map/all_to_all | solution.py:30
  17.8 105.9 %all-reduce.9.cloned.1.call-start = ((), (), s32[]{:S(2)}) async-start(), calls=%async_computation.3 | async-start | bytes 262144 | tf_op jit(solution)/shard_map/psum | solution.py:266
  20.9 11.8 %copy-start.19 = (f32[384,256]{1,0:T(8,128)}, f32[384,256]{1,0:T(8,128)S(1)}, u32[]{:S(2)}) copy-start(f32[384,256]{1,0:T(8,128)S(1)} %get-tuple-element.107.refs_2_) | copy-start | bytes 1179652
  21.7 12.2 %copy-start.67 = (s32[1,1,4,384]{3,2,1,0:T(4,128)S(1)}, s32[1,1,4,384]{3,2,1,0:T(4,128)}, u32[]{:S(2)}) copy-start(s32[1,1,4,384]{3,2,1,0:T(4,128)} %param.14) | copy-start | bytes 18436
  21.7 22.6 %collective-permute-start = (f32[416,256]{1,0:T(8,128)}, f32[416,256]{1,0:T(8,128)S(1)}, u32[]{:S(2)}, u32[]{:S(2)}) collective-permute-start(f32[416,256]{1,0:T(8,128)} %pad_maximum_fusion.1), channel_id=1, source_target_pairs={{0,1},{1,2},{2,3},{3,4},{4,5},{5,6},{6,7},{8,9},{9,10},{10,11},{11... | collective-permute-start | bytes 1277960 | tf_op jit(solution)/shard_map/ppermute | solution.py:20
  26.3 19.3 %collective-permute-start.1 = (f32[416,256]{1,0:T(8,128)}, f32[416,256]{1,0:T(8,128)}, u32[]{:S(2)}, u32[]{:S(2)}) collective-permute-start(f32[416,256]{1,0:T(8,128)} %pad_maximum_fusion.2), channel_id=1, source_target_pairs={{1,0},{2,1},{3,2},{4,3},{5,4},{6,5},{7,6},{9,8},{10,9},{11,10},{12... | collective-permute-start | bytes 1277960 | tf_op jit(solution)/shard_map/ppermute | solution.py:20
  28.4 19.4 %collective-permute-start.2 = (f32[416,256]{1,0:T(8,128)}, f32[416,256]{1,0:T(8,128)}, u32[]{:S(2)}, u32[]{:S(2)}) collective-permute-start(f32[416,256]{1,0:T(8,128)} %pad_maximum_fusion.3), channel_id=1, source_target_pairs={{0,8},{8,16},{16,24},{1,9},{9,17},{17,25},{2,10},{10,18},{18,26},{... | collective-permute-start | bytes 1277960 | tf_op jit(solution)/shard_map/ppermute | solution.py:20
  32.6 17.5 %collective-permute-start.3 = (f32[416,256]{1,0:T(8,128)}, f32[416,256]{1,0:T(8,128)}, u32[]{:S(2)}, u32[]{:S(2)}) collective-permute-start(f32[416,256]{1,0:T(8,128)} %pad_maximum_fusion.4), channel_id=1, source_target_pairs={{8,0},{16,8},{24,16},{9,1},{17,9},{25,17},{10,2},{18,10},{26,18},{... | collective-permute-start | bytes 1277960 | tf_op jit(solution)/shard_map/ppermute | solution.py:20
  50.1 12.3 %copy-start.61 = (f32[128,384]{1,0:T(8,128)}, f32[128,384]{1,0:T(8,128)S(1)}, u32[]{:S(2)}) copy-start(f32[128,384]{1,0:T(8,128)S(1)} %fusion.37) | copy-start | bytes 589828
  52.7 35.5 %copy-start.57 = (f32[128,1536]{1,0:T(8,128)}, f32[128,1536]{1,0:T(8,128)S(1)}, u32[]{:S(2)}) copy-start(f32[128,1536]{1,0:T(8,128)S(1)} %broadcast_multiply_fusion) | copy-start | bytes 2359300
  72.5 16.8 %copy-start.3 = (f32[384,256]{1,0:T(8,128)}, f32[384,256]{1,0:T(8,128)S(1)}, u32[]{:S(2)}) copy-start(f32[384,256]{1,0:T(8,128)S(1)} %get-tuple-element.51.refs_2_) | copy-start | bytes 1179652
  72.6 16.8 %copy-start.5 = (f32[384,256]{1,0:T(8,128)}, f32[384,256]{1,0:T(8,128)S(1)}, u32[]{:S(2)}) copy-start(f32[384,256]{1,0:T(8,128)S(1)} %get-tuple-element.52.refs_3_) | copy-start | bytes 1179652
  72.6 137.5 %copy-start.7 = (f32[384,256]{1,0:T(8,128)}, f32[384,256]{1,0:T(8,128)S(1)}, u32[]{:S(2)}) copy-start(f32[384,256]{1,0:T(8,128)S(1)} %get-tuple-element.58.refs_3_) | copy-start | bytes 1179652
  72.6 137.5 %copy-start.9 = (f32[384,256]{1,0:T(8,128)}, f32[384,256]{1,0:T(8,128)S(1)}, u32[]{:S(2)}) copy-start(f32[384,256]{1,0:T(8,128)S(1)} %get-tuple-element.57.refs_2_) | copy-start | bytes 1179652
  76.9 124.1 %collective-permute-start.4 = (f32[384,256]{1,0:T(8,128)}, f32[384,256]{1,0:T(8,128)}, u32[]{:S(2)}, u32[]{:S(2)}) collective-permute-start(f32[384,256]{1,0:T(8,128)} %get-tuple-element.54.refs_3_), channel_id=1, source_target_pairs={{0,8},{8,16},{16,24},{1,9},{9,17},{17,25},{2,10},{10,18},{18,26},{... | collective-permute-start | bytes 1179656 | tf_op jit(solution)/shard_map/ppermute | solution.py:20
  79.2 130.8 %collective-permute-start.6 = (f32[384,256]{1,0:T(8,128)S(1)}, f32[384,256]{1,0:T(8,128)}, u32[]{:S(2)}, u32[]{:S(2)}) collective-permute-start(f32[384,256]{1,0:T(8,128)S(1)} %get-tuple-element.58.refs_3_), channel_id=1, source_target_pairs={{0,1},{1,2},{2,3},{3,4},{4,5},{5,6},{6,7},{8,9},{9,10},{10,11},{11... | collective-permute-start | bytes 1179656 | tf_op jit(solution)/shard_map/ppermute | solution.py:20
  84.2 116.7 %collective-permute-start.5 = (f32[384,256]{1,0:T(8,128)}, f32[384,256]{1,0:T(8,128)}, u32[]{:S(2)}, u32[]{:S(2)}) collective-permute-start(f32[384,256]{1,0:T(8,128)} %get-tuple-element.53.refs_2_), channel_id=1, source_target_pairs={{8,0},{16,8},{24,16},{9,1},{17,9},{25,17},{10,2},{18,10},{26,18},{... | collective-permute-start | bytes 1179656 | tf_op jit(solution)/shard_map/ppermute | solution.py:20
  86.9 123.2 %collective-permute-start.7 = (f32[384,256]{1,0:T(8,128)S(1)}, f32[384,256]{1,0:T(8,128)}, u32[]{:S(2)}, u32[]{:S(2)}) collective-permute-start(f32[384,256]{1,0:T(8,128)S(1)} %get-tuple-element.57.refs_2_), channel_id=1, source_target_pairs={{1,0},{2,1},{3,2},{4,3},{5,4},{6,5},{7,6},{9,8},{10,9},{11,10},{12... | collective-permute-start | bytes 1179656 | tf_op jit(solution)/shard_map/ppermute | solution.py:20
  89.1 108.0 %all-reduce.11.cloned.1.call-start = ((), (), s32[]{:S(2)}) async-start(), calls=%async_computation.4 | async-start | bytes 262144 | tf_op jit(solution)/shard_map/psum | solution.py:266
  91.4 107.6 %copy-start.65 = (f32[128,1536]{1,0:T(8,128)S(1)}, f32[128,1536]{1,0:T(8,128)}, u32[]{:S(2)}) copy-start(f32[128,1536]{1,0:T(8,128)} %fusion.77) | copy-start | bytes 2359300
  210.0 68.9 %copy-start.31 = (f32[384,256]{1,0:T(8,128)}, f32[384,256]{1,0:T(8,128)S(1)}, u32[]{:S(2)}) copy-start(f32[384,256]{1,0:T(8,128)S(1)} %get-tuple-element.55.refs_8_.refs_0_) | copy-start | bytes 1179652
  217.3 24.6 %copy-start.23 = (f32[384,256]{1,0:T(8,128)}, f32[384,256]{1,0:T(8,128)S(1)}, u32[]{:S(2)}) copy-start(f32[384,256]{1,0:T(8,128)S(1)} %get-tuple-element.64.refs_2_) | copy-start | bytes 1179652
  217.3 24.6 %copy-start.25 = (f32[384,256]{1,0:T(8,128)}, f32[384,256]{1,0:T(8,128)S(1)}, u32[]{:S(2)}) copy-start(f32[384,256]{1,0:T(8,128)S(1)} %get-tuple-element.65.refs_3_) | copy-start | bytes 1179652
  217.3 24.5 %collective-permute-start.10 = (f32[384,256]{1,0:T(8,128)S(1)}, f32[384,256]{1,0:T(8,128)S(1)}, u32[]{:S(2)}, u32[]{:S(2)}) collective-permute-start(f32[384,256]{1,0:T(8,128)S(1)} %get-tuple-element.65.refs_3_), channel_id=1, source_target_pairs={{0,8},{8,16},{16,24},{1,9},{9,17},{17,25},{2,10},{10,18},{18,26},{... | collective-permute-start | bytes 1179656 | tf_op jit(solution)/shard_map/ppermute | solution.py:20
  218.6 23.2 %collective-permute-start.11 = (f32[384,256]{1,0:T(8,128)S(1)}, f32[384,256]{1,0:T(8,128)}, u32[]{:S(2)}, u32[]{:S(2)}) collective-permute-start(f32[384,256]{1,0:T(8,128)S(1)} %get-tuple-element.64.refs_2_), channel_id=1, source_target_pairs={{8,0},{16,8},{24,16},{9,1},{17,9},{25,17},{10,2},{18,10},{26,18},{... | collective-permute-start | bytes 1179656 | tf_op jit(solution)/shard_map/ppermute | solution.py:20
  224.6 15.7 %all-to-all-start.1 = ((f32[32,2,256]{2,1,0:T(2,128)}), f32[32,2,256]{2,1,0:T(2,128)}, u32[]{:S(2)}, u32[]{:S(2)}) async-start(f32[32,2,256]{2,1,0:T(2,128)} %broadcast_in_dim.31), calls=%async_computation.1 | async-start | bytes 131072 | tf_op jit(solution)/shard_map/all_to_all | solution.py:30
  234.7 21.0 %collective-permute-start.8 = (f32[384,256]{1,0:T(8,128)}, f32[384,256]{1,0:T(8,128)}, u32[]{:S(2)}, u32[]{:S(2)}) collective-permute-start(f32[384,256]{1,0:T(8,128)} %get-tuple-element.63.refs_3_), channel_id=1, source_target_pairs={{0,1},{1,2},{2,3},{3,4},{4,5},{5,6},{6,7},{8,9},{9,10},{10,11},{11... | collective-permute-start | bytes 1179656 | tf_op jit(solution)/shard_map/ppermute | solution.py:20
  239.0 16.7 %collective-permute-start.9 = (f32[384,256]{1,0:T(8,128)}, f32[384,256]{1,0:T(8,128)}, u32[]{:S(2)}, u32[]{:S(2)}) collective-permute-start(f32[384,256]{1,0:T(8,128)} %get-tuple-element.62.refs_2_), channel_id=1, source_target_pairs={{1,0},{2,1},{3,2},{4,3},{5,4},{6,5},{7,6},{9,8},{10,9},{11,10},{12... | collective-permute-start | bytes 1179656 | tf_op jit(solution)/shard_map/ppermute | solution.py:20
  245.6 15.8 %slice-start.3 = ((s8[9437184]{0:T(1024)(128)(4,1)}), s8[4194304]{0:T(1024)(128)(4,1)S(1)}, s32[]{:S(2)}) async-start(s8[9437184]{0:T(1024)(128)(4,1)} %bitcast.81), calls=%async_computation.10 | async-start | bytes 8388608
  245.6 15.8 %slice-start.4 = ((s8[9437184]{0:T(1024)(128)(4,1)}), s8[1048576]{0:T(1024)(128)(4,1)S(1)}, s32[]{:S(2)}) async-start(s8[9437184]{0:T(1024)(128)(4,1)} %bitcast.81), calls=%async_computation.11 | async-start | bytes 2097152
  250.5 23.8 %copy-start.37 = (f32[384,256]{1,0:T(8,128)}, f32[384,256]{1,0:T(8,128)S(1)}, u32[]{:S(2)}) copy-start(f32[384,256]{1,0:T(8,128)S(1)} %get-tuple-element.80) | copy-start | bytes 1179652
  250.5 23.8 %copy-start.39 = (f32[384,256]{1,0:T(8,128)}, f32[384,256]{1,0:T(8,128)S(1)}, u32[]{:S(2)}) copy-start(f32[384,256]{1,0:T(8,128)S(1)} %get-tuple-element.81) | copy-start | bytes 1179652
  261.3 13.0 %copy-start.27 = (f32[384,256]{1,0:T(8,128)}, f32[384,256]{1,0:T(8,128)S(1)}, u32[]{:S(2)}) copy-start(f32[384,256]{1,0:T(8,128)S(1)} %get-tuple-element.67.refs_2_) | copy-start | bytes 1179652
  261.3 16.6 %copy-start.29 = (f32[384,256]{1,0:T(8,128)}, f32[384,256]{1,0:T(8,128)S(1)}, u32[]{:S(2)}) copy-start(f32[384,256]{1,0:T(8,128)S(1)} %get-tuple-element.68.refs_3_) | copy-start | bytes 1179652
  261.3 25.1 %copy-start.36 = (f32[384,256]{1,0:T(8,128)}, f32[384,256]{1,0:T(8,128)S(1)}, u32[]{:S(2)}) copy-start(f32[384,256]{1,0:T(8,128)S(1)} %get-tuple-element.75.refs_2_) | copy-start | bytes 1179652
  261.4 13.0 %copy-start.55 = (f32[1536,256]{1,0:T(8,128)S(1)}, f32[1536,256]{1,0:T(8,128)}, u32[]{:S(2)}) copy-start(f32[1536,256]{1,0:T(8,128)} %fusion.33) | copy-start | bytes 4718596
  263.8 15.1 %collective-permute-start.12 = (f32[384,256]{1,0:T(8,128)S(1)}, f32[384,256]{1,0:T(8,128)S(1)}, u32[]{:S(2)}, u32[]{:S(2)}) collective-permute-start(f32[384,256]{1,0:T(8,128)S(1)} %get-tuple-element.70.refs_3_), channel_id=1, source_target_pairs={{0,8},{8,16},{16,24},{1,9},{9,17},{17,25},{2,10},{10,18},{18,26},{... | collective-permute-start | bytes 1179656 | tf_op jit(solution)/shard_map/ppermute | solution.py:20
  266.2 18.8 %collective-permute-start.14 = (f32[384,256]{1,0:T(8,128)S(1)}, f32[384,256]{1,0:T(8,128)S(1)}, u32[]{:S(2)}, u32[]{:S(2)}) collective-permute-start(f32[384,256]{1,0:T(8,128)S(1)} %get-tuple-element.76.refs_3_), channel_id=1, source_target_pairs={{0,1},{1,2},{2,3},{3,4},{4,5},{5,6},{6,7},{8,9},{9,10},{10,11},{11... | collective-permute-start | bytes 1179656 | tf_op jit(solution)/shard_map/ppermute | solution.py:20
  270.6 8.3 %collective-permute-start.13 = (f32[384,256]{1,0:T(8,128)S(1)}, f32[384,256]{1,0:T(8,128)S(1)}, u32[]{:S(2)}, u32[]{:S(2)}) collective-permute-start(f32[384,256]{1,0:T(8,128)S(1)} %get-tuple-element.69.refs_2_), channel_id=1, source_target_pairs={{8,0},{16,8},{24,16},{9,1},{17,9},{25,17},{10,2},{18,10},{26,18},{... | collective-permute-start | bytes 1179656 | tf_op jit(solution)/shard_map/ppermute | solution.py:20
  272.8 13.6 %collective-permute-start.15 = (f32[384,256]{1,0:T(8,128)S(1)}, f32[384,256]{1,0:T(8,128)S(1)}, u32[]{:S(2)}, u32[]{:S(2)}) collective-permute-start(f32[384,256]{1,0:T(8,128)S(1)} %get-tuple-element.75.refs_2_), channel_id=1, source_target_pairs={{1,0},{2,1},{3,2},{4,3},{5,4},{6,5},{7,6},{9,8},{10,9},{11,10},{12... | collective-permute-start | bytes 1179656 | tf_op jit(solution)/shard_map/ppermute | solution.py:20
  284.9 11.8 %copy-start.49 = (f32[384,256]{1,0:T(8,128)}, f32[384,256]{1,0:T(8,128)S(1)}, u32[]{:S(2)}) copy-start(f32[384,256]{1,0:T(8,128)S(1)} %get-tuple-element.73.refs_4_) | copy-start | bytes 1179652
  298.3 53.9 %all-to-all-start.2 = ((f32[32,3,256]{2,1,0:T(4,128)}), f32[32,3,256]{2,1,0:T(4,128)}, u32[]{:S(2)}, u32[]{:S(2)}) async-start(f32[32,3,256]{2,1,0:T(4,128)} %broadcast_in_dim.33), calls=%async_computation.2 | async-start | bytes 262144 | tf_op jit(solution)/shard_map/all_to_all | solution.py:30
  307.5 35.7 %all-reduce.13.cloned.1.call-start = ((), (), s32[]{:S(2)}) async-start(), calls=%async_computation.5 | async-start | bytes 262144 | tf_op jit(solution)/shard_map/psum | solution.py:266
  309.7 110.4 %all-reduce.15.cloned.1.call-start = ((), (), s32[]{:S(2)}) async-start(), calls=%async_computation.6 | async-start | bytes 262144 | tf_op jit(solution)/shard_map/psum | solution.py:266
  343.3 83.7 %collective-permute-start.16 = (f32[384,256]{1,0:T(8,128)}, f32[384,256]{1,0:T(8,128)}, u32[]{:S(2)}, u32[]{:S(2)}) collective-permute-start(f32[384,256]{1,0:T(8,128)} %copy-done.47), channel_id=1, source_target_pairs={{0,8},{8,16},{16,24},{1,9},{9,17},{17,25},{2,10},{10,18},{18,26},{... | collective-permute-start | bytes 1179656 | tf_op jit(solution)/shard_map/ppermute | solution.py:20
  345.4 81.7 %collective-permute-start.17 = (f32[384,256]{1,0:T(8,128)}, f32[384,256]{1,0:T(8,128)}, u32[]{:S(2)}, u32[]{:S(2)}) collective-permute-start(f32[384,256]{1,0:T(8,128)} %copy-done.45), channel_id=1, source_target_pairs={{8,0},{16,8},{24,16},{9,1},{17,9},{25,17},{10,2},{18,10},{26,18},{... | collective-permute-start | bytes 1179656 | tf_op jit(solution)/shard_map/ppermute | solution.py:20
  346.6 80.4 %collective-permute-start.18 = (f32[384,256]{1,0:T(8,128)}, f32[384,256]{1,0:T(8,128)}, u32[]{:S(2)}, u32[]{:S(2)}) collective-permute-start(f32[384,256]{1,0:T(8,128)} %copy-done.43), channel_id=1, source_target_pairs={{0,1},{1,2},{2,3},{3,4},{4,5},{5,6},{6,7},{8,9},{9,10},{10,11},{11... | collective-permute-start | bytes 1179656 | tf_op jit(solution)/shard_map/ppermute | solution.py:20
  350.8 76.2 %collective-permute-start.19 = (f32[384,256]{1,0:T(8,128)}, f32[384,256]{1,0:T(8,128)}, u32[]{:S(2)}, u32[]{:S(2)}) collective-permute-start(f32[384,256]{1,0:T(8,128)} %copy-done.41), channel_id=1, source_target_pairs={{1,0},{2,1},{3,2},{4,3},{5,4},{6,5},{7,6},{9,8},{10,9},{11,10},{12... | collective-permute-start | bytes 1179656 | tf_op jit(solution)/shard_map/ppermute | solution.py:20
  (61 other events, 340.4 us)
Sparse Core Ops, SparseCore 0:
  89.3 34.3 all-reduce.8
  127.4 69.7 all-reduce.10
  310.7 32.5 all-reduce.12
  346.8 73.2 all-reduce.14
